TPU v7x, 256 devices: a whole 4x4x8 slice. The times are simulated.
256 devices in a mesh: dp: 8 (over y, z_hi), tensor: 32 (over z_lo, x, core).
Axes of the slice: x: 4, y: 4, z: 8 (z_hi: 2, z_lo: 4; z = z_hi * 4 + z_lo), core: 2. Of those that a mesh axis runs over, the one named last changes fastest.
Arguments:
- inputs: float32 [1024, 4096], P('dp', 'tensor'), may hold values from -6 to 6
- out_grad: float32 [1024, 4096], P('dp', 'tensor'), may hold values from -6 to 6
- up_weight: float32 [768, 128, 128], P('tensor'), may hold values from -0.25 to 0.25
- down_weight: float32 [768, 128, 128], P('tensor'), may hold values from -0.109375 to 0.109375
- up_left: float32 [4096, 128], P('tensor'), may hold values from -0.09375 to 0.09375
- up_right: float32 [128, 16384], P(None, 'tensor'), may hold values from -0.5 to 0.5
- down_left: float32 [16384, 128], P('tensor'), may hold values from -0.046875 to 0.046875
- down_right: float32 [128, 4096], P(None, 'tensor'), may hold values from -0.5 to 0.5
- model_block: int32 [768], P('tensor'), may hold values from 0 to 31, as said below
- hidden_block: int32 [768], P('tensor'), may hold values from 0 to 3
- live_slots: int32 [32], P('tensor'), may hold values from 12 to 24, as said below
Outputs:
- result: float32 [1024, 4096], P('dp', 'tensor')
- input_grad: float32 [1024, 4096], P('dp', 'tensor')
- up_grad: float32 [768, 128, 128], P('tensor', 'dp')
- down_grad: float32 [768, 128, 128], P('tensor', 'dp')
- up_left_grad: float32 [4096, 128], P(('tensor', 'dp'))
- up_right_grad: float32 [128, 16384], P('dp', 'tensor')
- down_left_grad: float32 [16384, 128], P(('tensor', 'dp'))
- down_right_grad: float32 [128, 4096], P('dp', 'tensor')
Inputs may be any that keep to these rules, and one draw needn't show every extreme that they name: `model_block`: with g the slot's hidden block counted over all owners, the slot's model block differs from g mod 32 in at most one bit. `live_slots`: at least one owner has all 24 slots live.
All inputs are finite; a program needn't handle non-finite values.
Results may differ from a plain program's by a relative error of at most 0.0003.
Values sent between devices are 32-bit elements; how exact they have to be, the bound alone decides.
No kernel may reach another device: no remote copies, remote signals or barrier semaphores. Data moves between devices by JAX's collectives and lax.ppermute only.
A program may use at most 64 MiB of HBM per device.

v0:
```python
import jax
import jax.numpy as jnp
from jax import lax
from jax.experimental import pallas as pl
from jax.experimental.pallas import tpu as pltpu
from jax.sharding import PartitionSpec as P

f32 = jnp.float32
highest = lax.Precision.HIGHEST
VMEM = pl.BlockSpec(memory_space=pltpu.VMEM)
HBM = pl.BlockSpec(memory_space=pl.ANY)
SMEM = pl.BlockSpec(memory_space=pltpu.SMEM)
ROOT = 0.7978845608028654
CUBE = 0.044715
BATCH = 4

NN = ((1,), (0,))
NT = ((1,), (1,))
TN = ((0,), (0,))


def split(value):
    high = value.astype(jnp.bfloat16)
    return high, (value - high.astype(f32)).astype(jnp.bfloat16)


def dot3(left, right, dims):
    def one(a, b):
        return lax.dot_general(a, b, (dims, ((), ())), preferred_element_type=f32)

    return one(left[0], right[0]) + (one(left[0], right[1]) + one(left[1], right[0]))


def load(pairs, sems):
    copies = [pltpu.make_async_copy(a, b, sems.at[i]) for i, (a, b) in enumerate(pairs)]
    for copy in copies:
        copy.start()
    return copies


def hidden_kernel(
    model_ref, hidden_ref, live_ref, fields_hbm, up_hbm, down_hbm, low_ref, right_ref, left_ref,
    act_ref, pgrad_ref, part_ref, fields_ref, up_ref, down_ref, sems,
):
    rows = act_ref.shape[1]
    local_blocks = act_ref.shape[0]
    slot_count = up_ref.shape[0]
    copies = load([(fields_hbm, fields_ref), (up_hbm, up_ref), (down_hbm, down_ref)], sems)
    live = live_ref[0]
    low_in = split(low_ref[0:rows])
    back_mid = split(low_ref[rows : 2 * rows])
    for h in range(local_blocks):
        span = slice(h * 128, (h + 1) * 128)
        act_ref[h] = dot3(low_in, split(right_ref[:, span]), NN)
        pgrad_ref[h] = dot3(back_mid, split(left_ref[span]), NT)
    for copy in copies:
        copy.wait()

    @pl.loop(0, slot_count // BATCH)
    def _(step):
        terms = []
        for j in range(BATCH):
            s = step * BATCH + j
            m = model_ref[s]
            alive = jnp.where(s < live, 1.0, 0.0).astype(f32)
            up = dot3(split(fields_ref[m, 0:rows]), split(up_ref[s]), NN)
            back = dot3(split(fields_ref[m, rows : 2 * rows]), split(down_ref[s]), NT)
            terms.append((hidden_ref[s], up * alive, back * alive))
        for h, up, back in terms:
            act_ref[h] += up
            pgrad_ref[h] += back

    low_mid = None
    back_in = None
    for h in range(local_blocks):
        value = act_ref[h]
        square = value * value
        bent = jnp.tanh(ROOT * (value + CUBE * (value * square)))
        half = 0.5 * (1.0 + bent)
        slope = half + 0.5 * value * (1.0 - bent * bent) * (ROOT * (1.0 + 3.0 * CUBE * square))
        hidden = value * half
        pgrad = pgrad_ref[h] * slope
        act_ref[h] = hidden
        pgrad_ref[h] = pgrad
        span = slice(h * 128, (h + 1) * 128)
        mid = dot3(split(hidden), split(left_ref[span]), NN)
        back = dot3(split(pgrad), split(right_ref[:, span]), NT)
        low_mid = mid if low_mid is None else low_mid + mid
        back_in = back if back_in is None else back_in + back
    part_ref[0:rows] = low_mid
    part_ref[rows : 2 * rows] = back_in


def grads_kernel(
    model_ref, hidden_ref, live_ref, group_ref, fields_hbm, after_hbm, act_ref, pgrad_ref, low_ref,
    keep_up_ref, send_up_ref, keep_down_ref, send_down_ref, fields_ref, square_ref, tall_ref, sems,
):
    rows = act_ref.shape[1]
    local_blocks = act_ref.shape[0]
    slot_count = model_ref.shape[0]
    piece = keep_up_ref.shape[3]
    copies = load([(fields_hbm, fields_ref)], sems)
    live = live_ref[0]
    group = group_ref[0]
    low_in = split(low_ref[0:rows])
    back_mid = split(low_ref[rows : 2 * rows])

    def deal(keep_ref, send_ref, near, tile, source, stride, start):
        homes = {0: (keep_ref, 0), near ^ 2: (keep_ref, 1), near: (send_ref, 0), 2: (send_ref, 1)}
        for rel in range(8):
            ref, at = homes[rel >> 1]
            first = pl.multiple_of((group ^ rel) * stride + start, piece)
            ref[at, rel & 1, tile] = source[pl.ds(first, piece)]

    for h in range(local_blocks):
        square_ref[h] = dot3(low_in, split(pgrad_ref[h]), TN)
        deal(keep_up_ref, send_up_ref, 1, slot_count + h, square_ref.at[h], piece, 0)
        tall_ref[h * 128 : (h + 1) * 128] = dot3(split(act_ref[h]), back_mid, TN)
    for i in range(local_blocks):
        deal(keep_down_ref, send_down_ref, 3, slot_count + i, tall_ref, piece * local_blocks, piece * i)
    for copy in copies:
        copy.wait()

    @pl.loop(0, slot_count // BATCH)
    def _(step):
        for j in range(BATCH):
            s = step * BATCH + j
            m = model_ref[s]
            h = hidden_ref[s]
            alive = jnp.where(s < live, 1.0, 0.0).astype(f32)
            square_ref[2 * j] = dot3(split(fields_ref[m, 0:rows]), split(pgrad_ref[h]), TN) * alive
            square_ref[2 * j + 1] = dot3(split(act_ref[h]), split(fields_ref[m, rows : 2 * rows]), TN) * alive
        for j in range(BATCH):
            s = step * BATCH + j
            deal(keep_up_ref, send_up_ref, 1, s, square_ref.at[2 * j], piece, 0)
            deal(keep_down_ref, send_down_ref, 3, s, square_ref.at[2 * j + 1], piece, 0)


def terms_kernel(
    place_ref, hidden_ref, live_ref, up_hbm, down_hbm, act_ref, pgrad_ref,
    keep_ref, send_ref, up_ref, down_ref, sums, sems,
):
    rows = act_ref.shape[1]
    slot_count = up_ref.shape[0]
    copies = load([(up_hbm, up_ref), (down_hbm, down_ref)], sems)
    live = live_ref[0]
    for p in range(2):
        for b in range(16):
            sums[p, b] = jnp.zeros((rows, 128), f32)
    for copy in copies:
        copy.wait()

    @pl.loop(0, slot_count // BATCH)
    def _(step):
        terms = []
        for j in range(BATCH):
            s = step * BATCH + j
            h = hidden_ref[s]
            alive = jnp.where(s < live, 1.0, 0.0).astype(f32)
            out = dot3(split(act_ref[h]), split(down_ref[s]), NN) * alive
            back = dot3(split(pgrad_ref[h]), split(up_ref[s]), NT) * alive
            terms.append((place_ref[s], out, back))
        for b, out, back in terms:
            sums[0, b] += out
            sums[1, b] += back

    keep_ref[...] = sums[:, 0:8]
    send_ref[...] = sums[:, 8:16]


NEAR = (1, 3)


def core_kernel(first_ref, keep_ref, other_ref, hold_ref, send_out_ref, send_back_ref):
    first = first_ref[0]
    for p, send_ref in enumerate((send_out_ref, send_back_ref)):
        near = NEAR[p]
        homes = {0: (hold_ref.at[p], 0), near ^ 2: (hold_ref.at[p], 3), near: (send_ref, 0), 2: (send_ref, 3)}
        for e in range(4):
            ref, at = homes[e]
            ref[at] = keep_ref[p, e] + other_ref[p, e]
            mine = jnp.where(first == (e >> 1), 1.0, 0.0).astype(f32)
            for i in (1, 2):
                b = 2 + 2 * i + (e & 1)
                ref[at + i] = keep_ref[p, b] * mine + other_ref[p, b] * (1.0 - mine)


def near_kernel(hold_ref, got_out_ref, got_back_ref, stay_ref, send_out_ref, send_back_ref):
    for p, (got_ref, send_ref) in enumerate(((got_out_ref, send_out_ref), (got_back_ref, send_back_ref))):
        for f in range(4):
            for pair in range(2):
                total = hold_ref[p, 3 * pair + f] if f < 3 else None
                g = f ^ NEAR[p]
                if g < 3:
                    add = got_ref[3 * pair + g]
                    total = add if total is None else total + add
                if pair:
                    send_ref[f] = total
                else:
                    stay_ref[p, f] = total


def far_kernel(w_ref, stay_ref, got_out_ref, got_back_ref, hold_ref, send_ref):
    w = w_ref[0]
    for flip, ref, at in ((0, hold_ref, 0), (2, hold_ref, 1), (1, send_ref, 0), (3, send_ref, 1)):
        f = w ^ flip
        for p, got_ref in enumerate((got_out_ref, got_back_ref)):
            ref[at, p] = stay_ref[p, f] + got_ref[f ^ (NEAR[p] ^ 2)]


def y_kernel(keep_up_ref, got_up_ref, keep_down_ref, got_down_ref, after_hbm, hold_ref, send_up_ref, send_down_ref):
    hold_ref[0] = keep_up_ref[0] + got_up_ref[0]
    hold_ref[1] = keep_down_ref[0] + got_down_ref[0]
    send_up_ref[...] = keep_up_ref[1] + got_up_ref[1]
    send_down_ref[...] = keep_down_ref[1] + got_down_ref[1]


def ring_kernel(hold_ref, got_up_ref, got_down_ref, after_hbm, stay_ref, send_ref):
    for p, got_ref in enumerate((got_up_ref, got_down_ref)):
        stay_ref[p] = hold_ref[p, 0] + got_ref[0]
        send_ref[p] = hold_ref[p, 1] + got_ref[1]


def last_kernel(stay_ref, got_ref, up_ref, right_ref, down_ref, left_ref):
    slot_count, piece, _ = up_ref.shape
    up_ref[...] = stay_ref[0, 0:slot_count] + got_ref[0, 0:slot_count]
    down_ref[...] = stay_ref[1, 0:slot_count] + got_ref[1, 0:slot_count]
    for h in range(right_ref.shape[1] // 128):
        right_ref[:, h * 128 : (h + 1) * 128] = stay_ref[0, slot_count + h] + got_ref[0, slot_count + h]
        left_ref[h * piece : (h + 1) * piece] = stay_ref[1, slot_count + h] + got_ref[1, slot_count + h]


def ends_kernel(inputs_ref, grad_ref, low_ref, after_hbm, out_ref):
    parts, _, piece, _ = out_ref.shape
    rows = inputs_ref.shape[0]
    left = dot3(split(inputs_ref[...]), split(low_ref[rows : 2 * rows]), TN)
    right = dot3(split(low_ref[0:rows]), split(grad_ref[...]), TN)
    out_ref[:, 0] = left.reshape(parts, piece, 128)
    out_ref[:, 1] = right.reshape(parts, piece, 128)


def call(kernel, name, in_specs, outs, scratch=(), mflops=1, kbytes=1000):
    limit = (54 if name == "hidden" else 48 if scratch else 24) * 1024 * 1024
    return pl.pallas_call(
        kernel,
        out_shape=tuple(jax.ShapeDtypeStruct(shape, f32) for shape in outs),
        in_specs=in_specs,
        out_specs=(VMEM,) * len(outs),
        scratch_shapes=list(scratch),
        compiler_params=pltpu.CompilerParams(vmem_limit_bytes=limit),
        cost_estimate=pl.CostEstimate(flops=mflops * 10**6, bytes_accessed=kbytes * 10**3, transcendentals=0),
        name=name,
    )


def xor_shift(value, bits, axis="tensor"):
    return lax.ppermute(value, axis, [(i, i ^ bits) for i in range(lax.axis_size(axis))])


def exchange(value):
    return lax.all_to_all(value, "tensor", 0, 0, tiled=True)


def low_pieces(partial_value):
    size = lax.axis_size("tensor")
    return exchange(partial_value.reshape(size, -1, 128)).sum(axis=0)


def low_whole(pieces):
    size = lax.axis_size("tensor")
    return exchange(jnp.broadcast_to(pieces[None], (size,) + pieces.shape)).reshape(-1, 128)


def shards(
    inputs, out_grad, up_weight, down_weight, up_left, up_right, down_left, down_right,
    model_block, hidden_block, live_slots,
):
    rows = inputs.shape[0]
    slot_count = up_weight.shape[0]
    local_blocks = up_right.shape[1] // 128
    parts = lax.axis_size("dp")
    piece = 128 // parts
    me = lax.axis_index("tensor").astype(jnp.int32)
    core, x, z = me & 1, (me >> 1) & 3, me >> 3
    e = ((model_block >> 1) & 3) ^ x
    zrel = (model_block >> 3) ^ x
    place = jnp.where(zrel == 0, e, 2 + 2 * zrel + (e & 1)) + 8 * ((model_block & 1) ^ core)

    fields = lax.all_gather(jnp.concatenate([inputs, out_grad]), "tensor")
    first_part = jnp.concatenate(
        [
            jnp.dot(inputs, up_left, precision=highest),
            lax.dot_general(out_grad, down_right, (NT, ((), ())), precision=highest),
        ]
    )
    low = low_whole(low_pieces(first_part))
    group = lax.axis_index("dp").astype(jnp.int32)[None]
    local = (local_blocks, rows, 128)
    act, pgrad, low_part = call(
        hidden_kernel,
        "hidden",
        [SMEM] * 3 + [HBM] * 3 + [VMEM] * 3,
        (local, local, (2 * rows, 128)),
        [
            pltpu.VMEM(fields.shape, f32),
            pltpu.VMEM(up_weight.shape, f32),
            pltpu.VMEM(down_weight.shape, f32),
            pltpu.SemaphoreType.DMA((3,)),
        ],
        2000,
        12000,
    )(model_block, hidden_block, live_slots, fields, up_weight, down_weight, low, up_right, down_left)
    keep, send = call(
        terms_kernel,
        "terms",
        [SMEM] * 3 + [HBM] * 2 + [VMEM] * 2,
        ((2, 8, rows, 128),) * 2,
        [
            pltpu.VMEM(up_weight.shape, f32),
            pltpu.VMEM(down_weight.shape, f32),
            pltpu.VMEM((2, 16, rows, 128), f32),
            pltpu.SemaphoreType.DMA((2,)),
        ],
        1500,
        12000,
    )(place, hidden_block, live_slots, up_weight, down_weight, act, pgrad)
    tiles = slot_count + local_blocks
    keep_up, send_up, keep_down, send_down = call(
        grads_kernel,
        "grads",
        [SMEM] * 4 + [HBM] * 2 + [VMEM] * 3,
        ((2, 2, tiles, piece, 128),) * 4,
        [
            pltpu.VMEM(fields.shape, f32),
            pltpu.VMEM((2 * BATCH, 128, 128), f32),
            pltpu.VMEM(down_left.shape, f32),
            pltpu.SemaphoreType.DMA((1,)),
        ],
        1500,
        12000,
    )(model_block, hidden_block, live_slots, group, fields, send, act, pgrad, low)
    got_up = xor_shift(send_up, NEAR[0] << 1, "dp")
    got_down = xor_shift(send_down, NEAR[1] << 1, "dp")
    pieces = low_pieces(low_part)
    other = xor_shift(send, 1)
    hold, send_out, send_back = call(
        core_kernel, "core", [SMEM] + [VMEM] * 2, ((2, 6, rows, 128), (6, rows, 128), (6, rows, 128))
    )(((x // 2) ^ core)[None], keep, other)
    got_out = xor_shift(send_out, NEAR[0] << 1)
    got_back = xor_shift(send_back, NEAR[1] << 1)
    half = (2, tiles, piece, 128)
    hold_grads, send_up, send_down = call(
        y_kernel, "ring_y", [VMEM] * 4 + [HBM], ((2,) + half, half, half)
    )(keep_up, got_up, keep_down, got_down, send_out)
    got_up = xor_shift(send_up, NEAR[1] << 1, "dp")
    got_down = xor_shift(send_down, NEAR[0] << 1, "dp")
    stay, send_out, send_back = call(
        near_kernel, "near", [VMEM] * 3, ((2, 4, rows, 128), (4, rows, 128), (4, rows, 128))
    )(hold, got_out, got_back)
    got_out = xor_shift(send_out, NEAR[1] << 1)
    got_back = xor_shift(send_back, NEAR[0] << 1)
    pair = (2, 2, rows, 128)
    hold, send = call(far_kernel, "far", [SMEM] + [VMEM] * 3, (pair, pair))((x ^ z)[None], stay, got_out, got_back)
    got = xor_shift(send, 1 << 3)
    stay_grads, send_grads = call(ring_kernel, "ring_far", [VMEM] * 3 + [HBM], (half, half))(
        hold_grads, got_up, got_down, send
    )
    got_grads = xor_shift(send_grads, 1, "dp")
    blocks = hold[0] + got[0] + xor_shift(hold[1] + got[1], 2 << 3)
    lows = low_whole(pieces)
    low_mid, back_in = lows[:rows], lows[rows:]
    (ends,) = call(ends_kernel, "ends", [VMEM] * 3 + [HBM], ((parts, 2, piece, 128),))(
        inputs, out_grad, lows, send_grads
    )
    ends = lax.all_to_all(ends, "dp", 0, 0, tiled=True).sum(axis=0)
    up_grad, up_right_grad, down_grad, down_left_grad = call(
        last_kernel,
        "last",
        [VMEM] * 2,
        ((slot_count, piece, 128), (piece, local_blocks * 128), (slot_count, piece, 128), (local_blocks * piece, 128)),
    )(stay_grads, got_grads)
    result = blocks[0] + jnp.dot(low_mid, down_right, precision=highest)
    input_grad = blocks[1] + lax.dot_general(back_in, up_left, (NT, ((), ())), precision=highest)
    return result, input_grad, up_grad, down_grad, ends[0], up_right_grad, down_left_grad, ends[1]


def solution(mesh):
    return jax.shard_map(
        shards,
        mesh=mesh,
        in_specs=(
            P("dp", "tensor"),
            P("dp", "tensor"),
            P("tensor", None, None),
            P("tensor", None, None),
            P("tensor", None),
            P(None, "tensor"),
            P("tensor", None),
            P(None, "tensor"),
            P("tensor"),
            P("tensor"),
            P("tensor"),
        ),
        out_specs=(
            P("dp", "tensor"),
            P("dp", "tensor"),
            P("tensor", "dp", None),
            P("tensor", "dp", None),
            P(("tensor", "dp"), None),
            P("dp", "tensor"),
            P(("tensor", "dp"), None),
            P("dp", "tensor"),
        ),
        check_vma=False,
    )
```

profile of v0, /device:TPU:4, one launch (start us, length us, event | category | flops | bytes accessed | tf_op | source)
XLA Modules:
  0.0 204.5 jit_solution(15380693670406091369)
XLA Ops:
  7.2 1.5 pad_maximum_fusion
  8.8 1.1 fusion.9
  9.9 1.0 fusion.8
  11.0 15.3 %all_to_all.25 = f32[32,8,128]{2,1,0:T(8,128)S(1)} all-to-all(f32[32,8,128]{2,1,0:T(8,128)S(1)} %maximum_bitcast_fusion), channel_id=1, replica_groups=mesh['dp'=8,'tensor'=32] {'tensor'}, dimensions={0} | all-to-all | bytes 262144 | tf_op jit(solution)/shard_map/all_to_all | solution.py:261
  27.0 6.0 %all-to-all-start.1 = ((f32[32,8,128]{2,1,0:T(8,128)}), f32[32,8,128]{2,1,0:T(8,128)S(1)}, u32[]{:S(2)}, u32[]{:S(2)}) async-start(f32[32,8,128]{2,1,0:T(8,128)} %broadcast_in_dim.23), calls=%async_computation.1 | async-start | bytes 262144 | tf_op jit(solution)/shard_map/all_to_all | solution.py:261
  33.7 6.3 %all-to-all-done.1 = f32[32,8,128]{2,1,0:T(8,128)S(1)} async-done(((f32[32,8,128]{2,1,0:T(8,128)}), f32[32,8,128]{2,1,0:T(8,128)S(1)}, u32[]{:S(2)}, u32[]{:S(2)}) %all-to-all-start.1) | async-done | bytes 131104 | tf_op jit(solution)/shard_map/all_to_all | solution.py:261
  40.0 36.2 %all-gather.3.cloned.1.call-done = f32[8192,128]{1,0:T(8,128)} async-done(((f32[256,128]{1,0:T(8,128)}), f32[8192,128]{1,0:T(8,128)}) %all-gather.3.cloned.1.call-update) | async-done | bytes 4194320 | tf_op jit(solution)/shard_map/all_gather | solution.py:289
  76.3 8.8 %hidden.1 = (f32[4,128,128]{2,1,0:T(8,128)}, f32[4,128,128]{2,1,0:T(8,128)}, f32[256,128]{1,0:T(8,128)}) custom-call(s32[24]{0:T(128)} %model_ref.3, s32[24]{0:T(128)} %hidden_ref.5, s32[1]{0:T(128)S(6)} %copy.19.live_ref, f32[32,256,128]{2,1,0:T(8,128)} %bitcast.44, f32[24,128,128]{2,1,0:T(8,128)} %up_hbm.3, f32[24,128,128]{2,1,0:T(8,128)} %down_hbm.3, ...), custom_call_target="tpu_custom_call" | custom-call | flops 2000000000 | bytes 12000000 | tf_op jit(solution)/shard_map/hidden/pallas_call | solution.py:299
  85.1 0.9 copy-done.17
  86.1 0.9 copy-done.19
  87.0 4.3 %terms.1 = (f32[2,8,128,128]{3,2,1,0:T(8,128)S(1)}, f32[2,8,128,128]{3,2,1,0:T(8,128)S(1)}) custom-call(s32[24]{0:T(128)S(1)} %fusion.7.place_ref, s32[24]{0:T(128)S(1)} %copy-done.23, s32[1]{0:T(128)S(6)} %copy.19.live_ref, f32[24,128,128]{2,1,0:T(8,128)S(1)} %copy-done.1, f32[24,128,128]{2,1,0:T(8,128)S(1)} %copy-done.2, f32[4,128,128]{2,1,0:T(8,128)S(1)} %copy-done.17, ...), custom_call_target="tpu_custom_call" | custom-call | flops 1500000000 | bytes 12000000 | tf_op jit(solution)/shard_map/terms/pallas_call | solution.py:313
  91.6 0.9 copy-done.18
  92.6 0.9 copy-done.20
  93.5 6.7 %grads.1 = (f32[2,2,28,16,128]{4,3,2,1,0:T(8,128)S(1)}, f32[2,2,28,16,128]{4,3,2,1,0:T(8,128)}, f32[2,2,28,16,128]{4,3,2,1,0:T(8,128)S(1)}, f32[2,2,28,16,128]{4,3,2,1,0:T(8,128)}) custom-call(s32[24]{0:T(128)S(1)} %copy-done.22, s32[24]{0:T(128)S(1)} %copy-done.23, s32[1]{0:T(128)S(6)} %copy.19.live_ref, s32[1]{0:T(128)} %bitcast.12.group_ref, ...), custom_call_target="tpu_custom_call" | custom-call | flops 1500000000 | bytes 12000000 | tf_op jit(solution)/shard_map/grads/pallas_call | solution.py:328
  100.3 0.9 copy-done.5
  101.2 0.9 copy-done.7
  102.2 1.6 collective-permute-start.7
  103.8 1.9 collective-permute-start.8
  105.7 1.0 core.1
  106.7 0.9 copy-done.9
  107.6 1.4 collective-permute-start.1
  109.0 0.7 collective-permute-start.2
  109.7 6.6 %all-to-all-start.2 = ((f32[32,8,128]{2,1,0:T(8,128)}), f32[32,8,128]{2,1,0:T(8,128)S(1)}, u32[]{:S(2)}, u32[]{:S(2)}) async-start(f32[32,8,128]{2,1,0:T(8,128)} %bitcast.8), calls=%async_computation.2 | async-start | bytes 262144 | tf_op jit(solution)/shard_map/all_to_all | solution.py:261
  116.3 8.7 %collective-permute-done.7.got_up_ref = f32[2,2,28,16,128]{4,3,2,1,0:T(8,128)} collective-permute-done((f32[2,2,28,16,128]{4,3,2,1,0:T(8,128)}, f32[2,2,28,16,128]{4,3,2,1,0:T(8,128)}, u32[]{:S(2)}, u32[]{:S(2)}) %collective-permute-start.7) | collective-permute-done | bytes 917536 | tf_op jit(solution)/shard_map/ppermute | solution.py:257
  125.0 2.5 %collective-permute-done.8.got_down_ref = f32[2,2,28,16,128]{4,3,2,1,0:T(8,128)} collective-permute-done((f32[2,2,28,16,128]{4,3,2,1,0:T(8,128)}, f32[2,2,28,16,128]{4,3,2,1,0:T(8,128)}, u32[]{:S(2)}, u32[]{:S(2)}) %collective-permute-start.8) | collective-permute-done | bytes 917536 | tf_op jit(solution)/shard_map/ppermute | solution.py:257
  127.5 1.2 copy-done.8
  128.7 2.5 %ring_y.1 = (f32[2,2,28,16,128]{4,3,2,1,0:T(8,128)S(1)}, f32[2,28,16,128]{3,2,1,0:T(8,128)}, f32[2,28,16,128]{3,2,1,0:T(8,128)}) custom-call(f32[2,2,28,16,128]{4,3,2,1,0:T(8,128)S(1)} %copy-done.6, f32[2,2,28,16,128]{4,3,2,1,0:T(8,128)} %collective-permute-done.7.got_up_ref, f32[2,2,28,16,128]{4,3,2,1,0:T(8,128)S(1)} %copy-done.8, ...), custom_call_target="tpu_custom_call" | custom-call | flops 1000000 | bytes 1000000 | tf_op jit(solution)/shard_map/ring_y/pallas_call | solution.py:352
  131.2 1.9 collective-permute-start.9
  133.2 0.7 copy-done.13
  133.9 1.0 copy-done.14
  134.9 1.8 near.1
  136.8 1.3 collective-permute-start.3
  138.1 1.3 collective-permute-start.4
  140.1 6.6 %all-to-all-start.3 = ((f32[32,8,128]{2,1,0:T(8,128)}), f32[32,8,128]{2,1,0:T(8,128)S(1)}, u32[]{:S(2)}, u32[]{:S(2)}) async-start(f32[32,8,128]{2,1,0:T(8,128)} %broadcast_in_dim.24), calls=%async_computation.3 | async-start | bytes 262144 | tf_op jit(solution)/shard_map/all_to_all | solution.py:261
  146.8 0.8 far.1
  147.6 0.7 copy-done.15
  148.3 1.5 collective-permute-start.5
  149.9 3.4 %all-to-all-done.3 = f32[32,8,128]{2,1,0:T(8,128)S(1)} async-done(((f32[32,8,128]{2,1,0:T(8,128)}), f32[32,8,128]{2,1,0:T(8,128)S(1)}, u32[]{:S(2)}, u32[]{:S(2)}) %all-to-all-start.3) | async-done | bytes 131104 | tf_op jit(solution)/shard_map/all_to_all | solution.py:261
  153.3 0.9 ends.1
  154.2 7.3 %all-to-all-start.4 = ((f32[8,2,16,128]{3,2,1,0:T(8,128)}), f32[8,2,16,128]{3,2,1,0:T(8,128)S(1)}, u32[]{:S(2)}, u32[]{:S(2)}) async-start(f32[8,2,16,128]{3,2,1,0:T(8,128)} %ends.1), calls=%async_computation.4 | async-start | bytes 262144 | tf_op jit(solution)/shard_map/all_to_all | solution.py:375
  161.8 6.0 %collective-permute-start.11 = (f32[2,28,16,128]{3,2,1,0:T(8,128)S(1)}, f32[2,28,16,128]{3,2,1,0:T(8,128)S(1)}, u32[]{:S(2)}, u32[]{:S(2)}) collective-permute-start(f32[2,28,16,128]{3,2,1,0:T(8,128)S(1)} %get-tuple-element.55.after_hbm), channel_id=1, source_target_pairs={{0,32},{32,0},{64,96},{96,64},{128,160},{160,128},{192,224},{224,1... | collective-permute-start | bytes 1376264 | tf_op jit(solution)/shard_map/ppermute | solution.py:257
  167.8 5.0 %all-to-all-done.4 = f32[8,2,16,128]{3,2,1,0:T(8,128)S(1)} async-done(((f32[8,2,16,128]{3,2,1,0:T(8,128)}), f32[8,2,16,128]{3,2,1,0:T(8,128)S(1)}, u32[]{:S(2)}, u32[]{:S(2)}) %all-to-all-start.4) | async-done | bytes 131104 | tf_op jit(solution)/shard_map/all_to_all | solution.py:375
  172.9 0.9 fusion
  173.8 4.1 %collective-permute-start.6 = (f32[2,128,128]{2,1,0:T(8,128)S(1)}, f32[2,128,128]{2,1,0:T(8,128)S(1)}, u32[]{:S(2)}, u32[]{:S(2)}) collective-permute-start(f32[2,128,128]{2,1,0:T(8,128)S(1)} %fusion), channel_id=1, source_target_pairs={{0,16},{1,17},{2,18},{3,19},{4,20},{5,21},{6,22},{7,23},{8,24},{9,... | collective-permute-start | bytes 393224 | tf_op jit(solution)/shard_map/ppermute | solution.py:257
  178.5 16.5 %collective-permute-done.6 = f32[2,128,128]{2,1,0:T(8,128)S(1)} collective-permute-done((f32[2,128,128]{2,1,0:T(8,128)S(1)}, f32[2,128,128]{2,1,0:T(8,128)S(1)}, u32[]{:S(2)}, u32[]{:S(2)}) %collective-permute-start.6) | collective-permute-done | bytes 131104 | tf_op jit(solution)/shard_map/ppermute | solution.py:257
  195.0 0.9 fusion.2
  195.9 0.9 fusion.4
  196.8 0.8 last.1
  (63 shorter events, 2.8 us)
Async XLA Ops:
  7.2 2.8 %copy-start = (f32[128,128]{1,0:T(8,128)S(1)}, f32[128,128]{1,0:T(8,128)}, u32[]{:S(2)}) copy-start(f32[128,128]{1,0:T(8,128)} %param.15) | copy-start | bytes 196612
  7.2 26.5 %copy-start.21 = (s32[24]{0:T(128)S(1)}, s32[24]{0:T(128)}, u32[]{:S(2)}) copy-start(s32[24]{0:T(128)} %model_ref.3) | copy-start | bytes 292
  7.2 69.1 %all-gather.3.cloned.1.call-start = ((), (), s32[]{:S(2)}) async-start(), calls=%async_computation.5 | async-start | bytes 4325376 | tf_op jit(solution)/shard_map/all_gather | solution.py:289
  27.0 13.0 %all-to-all-start.1 = ((f32[32,8,128]{2,1,0:T(8,128)}), f32[32,8,128]{2,1,0:T(8,128)S(1)}, u32[]{:S(2)}, u32[]{:S(2)}) async-start(f32[32,8,128]{2,1,0:T(8,128)} %broadcast_in_dim.23), calls=%async_computation.1 | async-start | bytes 262144 | tf_op jit(solution)/shard_map/all_to_all | solution.py:261
  40.0 36.3 %copy-start.3 = (f32[32,8,128]{2,1,0:T(8,128)}, f32[32,8,128]{2,1,0:T(8,128)S(1)}, u32[]{:S(2)}) copy-start(f32[32,8,128]{2,1,0:T(8,128)S(1)} %all-to-all-done.1) | copy-start | bytes 393220
  76.3 8.8 %copy-start.1 = (f32[24,128,128]{2,1,0:T(8,128)S(1)}, f32[24,128,128]{2,1,0:T(8,128)}, u32[]{:S(2)}) copy-start(f32[24,128,128]{2,1,0:T(8,128)} %up_hbm.3) | copy-start | bytes 4718596
  76.3 8.8 %copy-start.2 = (f32[24,128,128]{2,1,0:T(8,128)S(1)}, f32[24,128,128]{2,1,0:T(8,128)}, u32[]{:S(2)}) copy-start(f32[24,128,128]{2,1,0:T(8,128)} %down_hbm.3) | copy-start | bytes 4718596
  76.3 8.8 %copy-start.23 = (s32[24]{0:T(128)S(1)}, s32[24]{0:T(128)}, u32[]{:S(2)}) copy-start(s32[24]{0:T(128)} %hidden_ref.5) | copy-start | bytes 292
  85.1 1.0 copy-start.17
  86.1 0.9 copy-start.19
  87.0 4.6 %copy-start.4 = (f32[32,8,128]{2,1,0:T(8,128)S(1)}, f32[32,8,128]{2,1,0:T(8,128)}, u32[]{:S(2)}) copy-start(f32[32,8,128]{2,1,0:T(8,128)} %copy-done.3) | copy-start | bytes 393220
  87.0 4.6 %copy-start.22 = (s32[24]{0:T(128)S(1)}, s32[24]{0:T(128)}, u32[]{:S(2)}) copy-start(s32[24]{0:T(128)} %model_ref.3) | copy-start | bytes 292
  91.3 14.4 %collective-permute-start = (f32[2,8,128,128]{3,2,1,0:T(8,128)S(1)}, f32[2,8,128,128]{3,2,1,0:T(8,128)S(1)}, u32[]{:S(2)}, u32[]{:S(2)}) collective-permute-start(f32[2,8,128,128]{3,2,1,0:T(8,128)S(1)} %get-tuple-element.37.after_hbm), channel_id=1, source_target_pairs={{0,1},{1,0},{2,3},{3,2},{4,5},{5,4},{6,7},{7,6},{8,9},{9,8},{10,11... | collective-permute-start | bytes 3145736 | tf_op jit(solution)/shard_map/ppermute | solution.py:257
  91.6 1.0 copy-start.18
  92.6 0.9 copy-start.20
  100.3 0.9 copy-start.5
  101.2 0.9 copy-start.7
  102.2 22.8 %collective-permute-start.7 = (f32[2,2,28,16,128]{4,3,2,1,0:T(8,128)}, f32[2,2,28,16,128]{4,3,2,1,0:T(8,128)}, u32[]{:S(2)}, u32[]{:S(2)}) collective-permute-start(f32[2,2,28,16,128]{4,3,2,1,0:T(8,128)} %get-tuple-element.48), channel_id=1, source_target_pairs={{0,64},{32,96},{64,0},{96,32},{128,192},{160,224},{192,128},{224,1... | collective-permute-start | bytes 2752520 | tf_op jit(solution)/shard_map/ppermute | solution.py:257
  103.8 23.8 %collective-permute-start.8 = (f32[2,2,28,16,128]{4,3,2,1,0:T(8,128)}, f32[2,2,28,16,128]{4,3,2,1,0:T(8,128)}, u32[]{:S(2)}, u32[]{:S(2)}) collective-permute-start(f32[2,2,28,16,128]{4,3,2,1,0:T(8,128)} %get-tuple-element.50), channel_id=1, source_target_pairs={{0,192},{32,224},{64,128},{96,160},{128,64},{160,96},{192,0},{224,... | collective-permute-start | bytes 2752520 | tf_op jit(solution)/shard_map/ppermute | solution.py:257
  105.7 21.8 %copy-start.6 = (f32[2,2,28,16,128]{4,3,2,1,0:T(8,128)S(1)}, f32[2,2,28,16,128]{4,3,2,1,0:T(8,128)}, u32[]{:S(2)}) copy-start(f32[2,2,28,16,128]{4,3,2,1,0:T(8,128)} %copy-done.5) | copy-start | bytes 2752516
  106.7 0.9 copy-start.9
  107.6 25.6 %collective-permute-start.1 = (f32[6,128,128]{2,1,0:T(8,128)}, f32[6,128,128]{2,1,0:T(8,128)S(1)}, u32[]{:S(2)}, u32[]{:S(2)}) collective-permute-start(f32[6,128,128]{2,1,0:T(8,128)} %get-tuple-element.39.after_hbm), channel_id=1, source_target_pairs={{0,2},{1,3},{2,0},{3,1},{4,6},{5,7},{6,4},{7,5},{8,10},{9,11},{10,... | collective-permute-start | bytes 1179656 | tf_op jit(solution)/shard_map/ppermute | solution.py:257
  109.0 24.9 %collective-permute-start.2 = (f32[6,128,128]{2,1,0:T(8,128)}, f32[6,128,128]{2,1,0:T(8,128)}, u32[]{:S(2)}, u32[]{:S(2)}) collective-permute-start(f32[6,128,128]{2,1,0:T(8,128)} %get-tuple-element.40), channel_id=1, source_target_pairs={{0,6},{1,7},{2,4},{3,5},{4,2},{5,3},{6,0},{7,1},{8,14},{9,15},{10,... | collective-permute-start | bytes 1179656 | tf_op jit(solution)/shard_map/ppermute | solution.py:257
  109.7 29.7 %all-to-all-start.2 = ((f32[32,8,128]{2,1,0:T(8,128)}), f32[32,8,128]{2,1,0:T(8,128)S(1)}, u32[]{:S(2)}, u32[]{:S(2)}) async-start(f32[32,8,128]{2,1,0:T(8,128)} %bitcast.8), calls=%async_computation.2 | async-start | bytes 262144 | tf_op jit(solution)/shard_map/all_to_all | solution.py:261
  127.5 1.2 copy-start.8
  128.7 5.2 %copy-start.10 = (f32[2,6,128,128]{3,2,1,0:T(8,128)S(1)}, f32[2,6,128,128]{3,2,1,0:T(8,128)}, u32[]{:S(2)}) copy-start(f32[2,6,128,128]{3,2,1,0:T(8,128)} %copy-done.9) | copy-start | bytes 2359300
  131.2 18.5 %collective-permute-start.9 = (f32[2,28,16,128]{3,2,1,0:T(8,128)}, f32[2,28,16,128]{3,2,1,0:T(8,128)S(1)}, u32[]{:S(2)}, u32[]{:S(2)}) collective-permute-start(f32[2,28,16,128]{3,2,1,0:T(8,128)} %get-tuple-element.52), channel_id=1, source_target_pairs={{0,192},{32,224},{64,128},{96,160},{128,64},{160,96},{192,0},{224,... | collective-permute-start | bytes 1376264 | tf_op jit(solution)/shard_map/ppermute | solution.py:257
  133.2 16.6 %collective-permute-start.10 = (f32[2,28,16,128]{3,2,1,0:T(8,128)}, f32[2,28,16,128]{3,2,1,0:T(8,128)S(1)}, u32[]{:S(2)}, u32[]{:S(2)}) collective-permute-start(f32[2,28,16,128]{3,2,1,0:T(8,128)} %get-tuple-element.53), channel_id=1, source_target_pairs={{0,64},{32,96},{64,0},{96,32},{128,192},{160,224},{192,128},{224,1... | collective-permute-start | bytes 1376264 | tf_op jit(solution)/shard_map/ppermute | solution.py:257
  133.2 0.7 copy-start.13
  133.9 1.0 copy-start.14
  136.8 10.0 %collective-permute-start.3 = (f32[4,128,128]{2,1,0:T(8,128)}, f32[4,128,128]{2,1,0:T(8,128)S(1)}, u32[]{:S(2)}, u32[]{:S(2)}) collective-permute-start(f32[4,128,128]{2,1,0:T(8,128)} %get-tuple-element.42), channel_id=1, source_target_pairs={{0,6},{1,7},{2,4},{3,5},{4,2},{5,3},{6,0},{7,1},{8,14},{9,15},{10,... | collective-permute-start | bytes 786440 | tf_op jit(solution)/shard_map/ppermute | solution.py:257
  138.1 8.7 %collective-permute-start.4 = (f32[4,128,128]{2,1,0:T(8,128)}, f32[4,128,128]{2,1,0:T(8,128)S(1)}, u32[]{:S(2)}, u32[]{:S(2)}) collective-permute-start(f32[4,128,128]{2,1,0:T(8,128)} %get-tuple-element.43), channel_id=1, source_target_pairs={{0,2},{1,3},{2,0},{3,1},{4,6},{5,7},{6,4},{7,5},{8,10},{9,11},{10,... | collective-permute-start | bytes 786440 | tf_op jit(solution)/shard_map/ppermute | solution.py:257
  140.1 13.2 %all-to-all-start.3 = ((f32[32,8,128]{2,1,0:T(8,128)}), f32[32,8,128]{2,1,0:T(8,128)S(1)}, u32[]{:S(2)}, u32[]{:S(2)}) async-start(f32[32,8,128]{2,1,0:T(8,128)} %broadcast_in_dim.24), calls=%async_computation.3 | async-start | bytes 262144 | tf_op jit(solution)/shard_map/all_to_all | solution.py:261
  146.8 6.5 %copy-start.11 = (f32[128,128]{1,0:T(8,128)S(1)}, f32[128,128]{1,0:T(8,128)}, u32[]{:S(2)}) copy-start(f32[128,128]{1,0:T(8,128)} %grad_ref.1) | copy-start | bytes 196612
  146.8 6.5 %copy-start.12 = (f32[128,128]{1,0:T(8,128)S(1)}, f32[128,128]{1,0:T(8,128)}, u32[]{:S(2)}) copy-start(f32[128,128]{1,0:T(8,128)} %inputs_ref.1) | copy-start | bytes 196612
  147.6 0.7 copy-start.15
  148.3 24.6 %collective-permute-start.5 = (f32[2,2,128,128]{3,2,1,0:T(8,128)}, f32[2,2,128,128]{3,2,1,0:T(8,128)}, u32[]{:S(2)}, u32[]{:S(2)}) collective-permute-start(f32[2,2,128,128]{3,2,1,0:T(8,128)} %get-tuple-element.45.after_hbm), channel_id=1, source_target_pairs={{0,8},{1,9},{2,10},{3,11},{4,12},{5,13},{6,14},{7,15},{8,0},{9,1},... | collective-permute-start | bytes 786440 | tf_op jit(solution)/shard_map/ppermute | solution.py:257
  149.8 11.8 %copy-start.24 = (f32[128,128]{1,0:T(8,128)S(1)}, f32[128,128]{1,0:T(8,128)}, u32[]{:S(2)}) copy-start(f32[128,128]{1,0:T(8,128)} %param.18) | copy-start | bytes 196612
  149.8 23.1 %copy-start.16 = (f32[2,2,128,128]{3,2,1,0:T(8,128)S(1)}, f32[2,2,128,128]{3,2,1,0:T(8,128)}, u32[]{:S(2)}) copy-start(f32[2,2,128,128]{3,2,1,0:T(8,128)} %copy-done.15) | copy-start | bytes 786436
  154.2 18.6 %all-to-all-start.4 = ((f32[8,2,16,128]{3,2,1,0:T(8,128)}), f32[8,2,16,128]{3,2,1,0:T(8,128)S(1)}, u32[]{:S(2)}, u32[]{:S(2)}) async-start(f32[8,2,16,128]{3,2,1,0:T(8,128)} %ends.1), calls=%async_computation.4 | async-start | bytes 262144 | tf_op jit(solution)/shard_map/all_to_all | solution.py:375
  161.8 35.0 %collective-permute-start.11 = (f32[2,28,16,128]{3,2,1,0:T(8,128)S(1)}, f32[2,28,16,128]{3,2,1,0:T(8,128)S(1)}, u32[]{:S(2)}, u32[]{:S(2)}) collective-permute-start(f32[2,28,16,128]{3,2,1,0:T(8,128)S(1)} %get-tuple-element.55.after_hbm), channel_id=1, source_target_pairs={{0,32},{32,0},{64,96},{96,64},{128,160},{160,128},{192,224},{224,1... | collective-permute-start | bytes 1376264 | tf_op jit(solution)/shard_map/ppermute | solution.py:257
  173.8 21.2 %collective-permute-start.6 = (f32[2,128,128]{2,1,0:T(8,128)S(1)}, f32[2,128,128]{2,1,0:T(8,128)S(1)}, u32[]{:S(2)}, u32[]{:S(2)}) collective-permute-start(f32[2,128,128]{2,1,0:T(8,128)S(1)} %fusion), channel_id=1, source_target_pairs={{0,16},{1,17},{2,18},{3,19},{4,20},{5,21},{6,22},{7,23},{8,24},{9,... | collective-permute-start | bytes 393224 | tf_op jit(solution)/shard_map/ppermute | solution.py:257
Sparse Core Ops, SparseCore 0:
  10.5 65.7 all-gather.2
where the time goes:
time: 209 us; the launch traced here: 204 us
  waiting for transfers between devices  78.8 us (38%)
  starting transfers between devices  48.7 us (23%)
  Pallas kernels  27.8 us (13%)
  blocking collectives  15.3 us (7%)
  between operations  15 us (7%)
  local copies, waits for them, and re-layouts  12.2 us (6%)
  other arithmetic  3.49 us (2%)
  matrix products  3.29 us (2%)
    all_gather x1, waiting for transfers between devices, shards(): fields = lax.all_gather(jnp.concatenate([inputs, out_grad]), 'tensor')  36.2 us
    ppermute x12, waiting for transfers between devices, xor_shift(): lax.ppermute(value, axis, [(i, i ^ bits) for i in range(lax.axis_size(axi...  27.7 us
    ppermute x12, starting transfers between devices, xor_shift(): lax.ppermute(value, axis, [(i, i ^ bits) for i in range(lax.axis_size(axi...  22 us
    all_to_all x3, starting transfers between devices, exchange(): return lax.all_to_all(value, 'tensor', 0, 0, tiled=True)  19.3 us
    all_to_all x1, blocking collectives, exchange(): return lax.all_to_all(value, 'tensor', 0, 0, tiled=True)  15.3 us
    unnamed x50, local copies, waits for them, and re-layouts  10.3 us
    all_to_all x3, waiting for transfers between devices, exchange(): return lax.all_to_all(value, 'tensor', 0, 0, tiled=True)  9.76 us
    pallas_call x1, Pallas kernels, shards(): call(hidden_kernel, 'hidden', [SMEM] * 3 + [HBM] * 3 + [VMEM] * 3, (local...  8.81 us
  transfers between devices with their start and end apart: 17, of which 7 were waited for; matrix products, arithmetic and copies ran while one was open for 4% of the time, Pallas kernels for 7%

commit v1 on v0

--- a/solution.py
+++ b/solution.py
@@ -171,7 +171,7 @@
 NEAR = (1, 3)
 
 
-def core_kernel(first_ref, keep_ref, other_ref, hold_ref, send_out_ref, send_back_ref):
+def core_kernel(first_ref, keep_ref, other_ref, after_hbm, hold_ref, send_out_ref, send_back_ref):
     first = first_ref[0]
     for p, send_ref in enumerate((send_out_ref, send_back_ref)):
         near = NEAR[p]
@@ -230,6 +230,12 @@
         left_ref[h * piece : (h + 1) * piece] = stay_ref[1, slot_count + h] + got_ref[1, slot_count + h]
 
 
+def pieces_kernel(parts_ref, after_hbm, out_ref):
+    total = jnp.sum(parts_ref[...], axis=0)
+    for i in range(out_ref.shape[0]):
+        out_ref[i] = total
+
+
 def ends_kernel(inputs_ref, grad_ref, low_ref, after_hbm, out_ref):
     parts, _, piece, _ = out_ref.shape
     rows = inputs_ref.shape[0]
@@ -240,7 +246,7 @@
 
 
 def call(kernel, name, in_specs, outs, scratch=(), mflops=1, kbytes=1000):
-    limit = (54 if name == "hidden" else 48 if scratch else 24) * 1024 * 1024
+    limit = (48 if scratch else 24) * 1024 * 1024
     return pl.pallas_call(
         kernel,
         out_shape=tuple(jax.ShapeDtypeStruct(shape, f32) for shape in outs),
@@ -341,36 +347,39 @@
     )(model_block, hidden_block, live_slots, group, fields, send, act, pgrad, low)
     got_up = xor_shift(send_up, NEAR[0] << 1, "dp")
     got_down = xor_shift(send_down, NEAR[1] << 1, "dp")
-    pieces = low_pieces(low_part)
+    size = lax.axis_size("tensor")
+    low_parts = exchange(low_part.reshape(size, -1, 128))
     other = xor_shift(send, 1)
     hold, send_out, send_back = call(
-        core_kernel, "core", [SMEM] + [VMEM] * 2, ((2, 6, rows, 128), (6, rows, 128), (6, rows, 128))
-    )(((x // 2) ^ core)[None], keep, other)
+        core_kernel, "core", [SMEM] + [VMEM] * 2 + [HBM], ((2, 6, rows, 128), (6, rows, 128), (6, rows, 128))
+    )(((x // 2) ^ core)[None], keep, other, send_up)
     got_out = xor_shift(send_out, NEAR[0] << 1)
     got_back = xor_shift(send_back, NEAR[1] << 1)
+    stay, send_out, send_back = call(
+        near_kernel, "near", [VMEM] * 3, ((2, 4, rows, 128), (4, rows, 128), (4, rows, 128))
+    )(hold, got_out, got_back)
     half = (2, tiles, piece, 128)
     hold_grads, send_up, send_down = call(
         y_kernel, "ring_y", [VMEM] * 4 + [HBM], ((2,) + half, half, half)
     )(keep_up, got_up, keep_down, got_down, send_out)
     got_up = xor_shift(send_up, NEAR[1] << 1, "dp")
     got_down = xor_shift(send_down, NEAR[0] << 1, "dp")
-    stay, send_out, send_back = call(
-        near_kernel, "near", [VMEM] * 3, ((2, 4, rows, 128), (4, rows, 128), (4, rows, 128))
-    )(hold, got_out, got_back)
     got_out = xor_shift(send_out, NEAR[1] << 1)
     got_back = xor_shift(send_back, NEAR[0] << 1)
     pair = (2, 2, rows, 128)
     hold, send = call(far_kernel, "far", [SMEM] + [VMEM] * 3, (pair, pair))((x ^ z)[None], stay, got_out, got_back)
     got = xor_shift(send, 1 << 3)
+    send = hold[1] + got[1]
     stay_grads, send_grads = call(ring_kernel, "ring_far", [VMEM] * 3 + [HBM], (half, half))(
         hold_grads, got_up, got_down, send
     )
     got_grads = xor_shift(send_grads, 1, "dp")
-    blocks = hold[0] + got[0] + xor_shift(hold[1] + got[1], 2 << 3)
-    lows = low_whole(pieces)
+    blocks = hold[0] + got[0] + xor_shift(send, 2 << 3)
+    (pieces,) = call(pieces_kernel, "pieces", [VMEM, HBM], (low_parts.shape,))(low_parts, send_up)
+    lows = exchange(pieces).reshape(-1, 128)
     low_mid, back_in = lows[:rows], lows[rows:]
     (ends,) = call(ends_kernel, "ends", [VMEM] * 3 + [HBM], ((parts, 2, piece, 128),))(
-        inputs, out_grad, lows, send_grads
+        inputs, out_grad, lows, blocks
     )
     ends = lax.all_to_all(ends, "dp", 0, 0, tiled=True).sum(axis=0)
     up_grad, up_right_grad, down_grad, down_left_grad = call(

time: 209 us -> 194 us (0.928)
  the two profiles are of different devices: /device:TPU:4 before, /device:TPU:66 now
where the time goes in v1:
time: 194 us
  waiting for transfers between devices  78.7 us (41%)
  starting transfers between devices  42.2 us (22%)
  Pallas kernels  24.9 us (13%)
  between operations  15 us (8%)
  blocking collectives  13.7 us (7%)
  local copies, waits for them, and re-layouts  11.3 us (6%)
  matrix products  4.12 us (2%)
  other arithmetic  3.71 us (2%)
    all_gather x1, waiting for transfers between devices, shards(): fields = lax.all_gather(jnp.concatenate([inputs, out_grad]), 'tensor')  36.4 us
    all_to_all x3, starting transfers between devices, exchange(): return lax.all_to_all(value, 'tensor', 0, 0, tiled=True)  20.6 us
    all_to_all x1, waiting for transfers between devices, shards(): ends = lax.all_to_all(ends, 'dp', 0, 0, tiled=True).sum(axis=0)  17.6 us
    ppermute x12, waiting for transfers between devices, xor_shift(): lax.ppermute(value, axis, [(i, i ^ bits) for i in range(lax.axis_size(axi...  16.8 us
    ppermute x12, starting transfers between devices, xor_shift(): lax.ppermute(value, axis, [(i, i ^ bits) for i in range(lax.axis_size(axi...  16.5 us
    all_to_all x1, blocking collectives, exchange(): return lax.all_to_all(value, 'tensor', 0, 0, tiled=True)  13.7 us
    unnamed x44, local copies, waits for them, and re-layouts  9.99 us
    all_to_all x3, waiting for transfers between devices, exchange(): return lax.all_to_all(value, 'tensor', 0, 0, tiled=True)  7.87 us
  transfers between devices with their start and end apart: 17, of which 8 were waited for; matrix products, arithmetic and copies ran while one was open for 4% of the time, Pallas kernels for 6%

profile of v1, /device:TPU:66, one launch (start us, length us, event | category | flops | bytes accessed | tf_op | source)
XLA Modules:
  0.0 193.6 jit_solution(17766984166626646876)
XLA Ops:
  7.3 1.7 pad_maximum_fusion
  9.0 1.0 fusion.8
  10.0 1.1 fusion.9
  11.2 13.7 %all_to_all.25 = f32[32,8,128]{2,1,0:T(8,128)S(1)} all-to-all(f32[32,8,128]{2,1,0:T(8,128)S(1)} %maximum_bitcast_fusion), channel_id=1, replica_groups=mesh['dp'=8,'tensor'=32] {'tensor'}, dimensions={0} | all-to-all | bytes 262144 | tf_op jit(solution)/shard_map/all_to_all | solution.py:267
  25.6 6.8 %all-to-all-start.1 = ((f32[32,8,128]{2,1,0:T(8,128)}), f32[32,8,128]{2,1,0:T(8,128)S(1)}, u32[]{:S(2)}, u32[]{:S(2)}) async-start(f32[32,8,128]{2,1,0:T(8,128)} %broadcast_in_dim.17), calls=%async_computation.1 | async-start | bytes 262144 | tf_op jit(solution)/shard_map/all_to_all | solution.py:267
  33.1 5.7 %all-to-all-done.1 = f32[32,8,128]{2,1,0:T(8,128)S(1)} async-done(((f32[32,8,128]{2,1,0:T(8,128)}), f32[32,8,128]{2,1,0:T(8,128)S(1)}, u32[]{:S(2)}, u32[]{:S(2)}) %all-to-all-start.1) | async-done | bytes 131104 | tf_op jit(solution)/shard_map/all_to_all | solution.py:267
  38.8 36.4 %all-gather.3.cloned.1.call-done = f32[8192,128]{1,0:T(8,128)} async-done(((f32[256,128]{1,0:T(8,128)}), f32[8192,128]{1,0:T(8,128)}) %all-gather.3.cloned.1.call-update) | async-done | bytes 4194320 | tf_op jit(solution)/shard_map/all_gather | solution.py:295
  75.2 1.4 copy-done.2
  76.6 0.9 copy-done.10
  77.5 7.2 %hidden.1 = (f32[4,128,128]{2,1,0:T(8,128)S(1)}, f32[4,128,128]{2,1,0:T(8,128)S(1)}, f32[256,128]{1,0:T(8,128)}) custom-call(s32[24]{0:T(128)S(1)} %copy-done.19, s32[24]{0:T(128)S(1)} %copy-done.20, s32[1]{0:T(128)S(6)} %copy.19.live_ref, f32[32,256,128]{2,1,0:T(8,128)} %bitcast.44, f32[24,128,128]{2,1,0:T(8,128)S(1)} %copy-done.1, ...), custom_call_target="tpu_custom_call" | custom-call | flops 2000000000 | bytes 12000000 | tf_op jit(solution)/shard_map/hidden/pallas_call | solution.py:305
  84.7 5.2 %terms.1 = (f32[2,8,128,128]{3,2,1,0:T(8,128)S(1)}, f32[2,8,128,128]{3,2,1,0:T(8,128)}) custom-call(s32[24]{0:T(128)S(1)} %fusion.7.place_ref, s32[24]{0:T(128)S(1)} %copy-done.20, s32[1]{0:T(128)S(6)} %copy.19.live_ref, f32[24,128,128]{2,1,0:T(8,128)S(1)} %copy-done.1, f32[24,128,128]{2,1,0:T(8,128)S(1)} %copy-done.2, ...), custom_call_target="tpu_custom_call" | custom-call | flops 1500000000 | bytes 12000000 | tf_op jit(solution)/shard_map/terms/pallas_call | solution.py:319
  90.2 6.7 %grads.1 = (f32[2,2,28,16,128]{4,3,2,1,0:T(8,128)S(1)}, f32[2,2,28,16,128]{4,3,2,1,0:T(8,128)}, f32[2,2,28,16,128]{4,3,2,1,0:T(8,128)S(1)}, f32[2,2,28,16,128]{4,3,2,1,0:T(8,128)}) custom-call(s32[24]{0:T(128)S(1)} %copy-done.19, s32[24]{0:T(128)S(1)} %copy-done.20, s32[1]{0:T(128)S(6)} %copy.19.live_ref, s32[1]{0:T(128)} %bitcast.5.group_ref, ...), custom_call_target="tpu_custom_call" | custom-call | flops 1500000000 | bytes 12000000 | tf_op jit(solution)/shard_map/grads/pallas_call | solution.py:334
  96.9 0.9 copy-done.3
  97.9 0.9 copy-done.5
  98.8 2.5 %collective-permute-start.8 = (f32[2,2,28,16,128]{4,3,2,1,0:T(8,128)}, f32[2,2,28,16,128]{4,3,2,1,0:T(8,128)}, u32[]{:S(2)}, u32[]{:S(2)}) collective-permute-start(f32[2,2,28,16,128]{4,3,2,1,0:T(8,128)} %get-tuple-element.50), channel_id=1, source_target_pairs={{0,192},{32,224},{64,128},{96,160},{128,64},{160,96},{192,0},{224,... | collective-permute-start | bytes 2752520 | tf_op jit(solution)/shard_map/ppermute | solution.py:263
  101.9 1.3 collective-permute-start.1
  103.2 0.7 collective-permute-start.2
  103.9 8.8 %collective-permute-done.1.got_out_ref = f32[6,128,128]{2,1,0:T(8,128)S(1)} collective-permute-done((f32[6,128,128]{2,1,0:T(8,128)S(1)}, f32[6,128,128]{2,1,0:T(8,128)S(1)}, u32[]{:S(2)}, u32[]{:S(2)}) %collective-permute-start.1) | collective-permute-done | bytes 393248 | tf_op jit(solution)/shard_map/ppermute | solution.py:263
  112.7 0.9 collective-permute-done.2.got_back_ref
  113.6 0.8 near.1
  114.4 2.0 %collective-permute-start.4 = (f32[4,128,128]{2,1,0:T(8,128)}, f32[4,128,128]{2,1,0:T(8,128)S(1)}, u32[]{:S(2)}, u32[]{:S(2)}) collective-permute-start(f32[4,128,128]{2,1,0:T(8,128)} %get-tuple-element.44), channel_id=1, source_target_pairs={{0,2},{1,3},{2,0},{3,1},{4,6},{5,7},{6,4},{7,5},{8,10},{9,11},{10,... | collective-permute-start | bytes 786440 | tf_op jit(solution)/shard_map/ppermute | solution.py:263
  116.5 1.0 collective-permute-start.3
  117.5 6.9 %all-to-all-start.2 = ((f32[32,8,128]{2,1,0:T(8,128)}), f32[32,8,128]{2,1,0:T(8,128)S(1)}, u32[]{:S(2)}, u32[]{:S(2)}) async-start(f32[32,8,128]{2,1,0:T(8,128)} %bitcast.9), calls=%async_computation.2 | async-start | bytes 262144 | tf_op jit(solution)/shard_map/all_to_all | solution.py:267
  124.4 0.7 copy-done.13
  125.1 0.7 copy-done.15
  125.8 0.9 copy-done.14
  126.7 0.9 copy-done.16
  127.7 0.8 far.1
  128.4 0.7 copy-done.11
  129.1 1.5 collective-permute-start.5
  130.7 0.9 copy-done.18
  131.6 1.6 ring_y.1
  133.3 0.8 copy-done.21
  134.1 0.7 pieces.1
  134.8 6.9 %all-to-all-start.3 = ((f32[32,8,128]{2,1,0:T(8,128)}), f32[32,8,128]{2,1,0:T(8,128)S(1)}, u32[]{:S(2)}, u32[]{:S(2)}) async-start(f32[32,8,128]{2,1,0:T(8,128)} %pieces.1), calls=%async_computation.3 | async-start | bytes 262144 | tf_op jit(solution)/shard_map/all_to_all | solution.py:267
  141.7 1.1 collective-permute-start.9
  142.8 0.9 collective-permute-start.10
  143.6 1.0 fusion.after_hbm
  145.3 2.2 %all-to-all-done.3 = f32[32,8,128]{2,1,0:T(8,128)S(1)} async-done(((f32[32,8,128]{2,1,0:T(8,128)}), f32[32,8,128]{2,1,0:T(8,128)S(1)}, u32[]{:S(2)}, u32[]{:S(2)}) %all-to-all-start.3) | async-done | bytes 131104 | tf_op jit(solution)/shard_map/all_to_all | solution.py:267
  147.4 1.0 fusion.5
  148.5 6.8 %collective-permute-done.10.got_down_ref = f32[2,28,16,128]{3,2,1,0:T(8,128)S(1)} collective-permute-done((f32[2,28,16,128]{3,2,1,0:T(8,128)}, f32[2,28,16,128]{3,2,1,0:T(8,128)S(1)}, u32[]{:S(2)}, u32[]{:S(2)}) %collective-permute-start.10) | collective-permute-done | bytes 458784 | tf_op jit(solution)/shard_map/ppermute | solution.py:263
  155.7 4.1 %collective-permute-start.11 = (f32[2,28,16,128]{3,2,1,0:T(8,128)S(1)}, f32[2,28,16,128]{3,2,1,0:T(8,128)S(1)}, u32[]{:S(2)}, u32[]{:S(2)}) collective-permute-start(f32[2,28,16,128]{3,2,1,0:T(8,128)S(1)} %get-tuple-element.55), channel_id=1, source_target_pairs={{0,32},{32,0},{64,96},{96,64},{128,160},{160,128},{192,224},{224,1... | collective-permute-start | bytes 1376264 | tf_op jit(solution)/shard_map/ppermute | solution.py:263
  159.8 1.0 fusion.2.after_hbm
  160.8 0.9 ends.1
  161.7 5.1 %all-to-all-start.4 = ((f32[8,2,16,128]{3,2,1,0:T(8,128)}), f32[8,2,16,128]{3,2,1,0:T(8,128)S(1)}, u32[]{:S(2)}, u32[]{:S(2)}) async-start(f32[8,2,16,128]{3,2,1,0:T(8,128)} %ends.1), calls=%async_computation.4 | async-start | bytes 262144 | tf_op jit(solution)/shard_map/all_to_all | solution.py:384
  166.9 0.9 fusion.4
  167.8 17.6 %all-to-all-done.4 = f32[8,2,16,128]{3,2,1,0:T(8,128)S(1)} async-done(((f32[8,2,16,128]{3,2,1,0:T(8,128)}), f32[8,2,16,128]{3,2,1,0:T(8,128)S(1)}, u32[]{:S(2)}, u32[]{:S(2)}) %all-to-all-start.4) | async-done | bytes 131104 | tf_op jit(solution)/shard_map/all_to_all | solution.py:384
  185.9 0.8 last.1
  (56 shorter events, 3.4 us)
Async XLA Ops:
  7.2 1.8 copy-start
  7.2 25.9 %copy-start.19 = (s32[24]{0:T(128)S(1)}, s32[24]{0:T(128)}, u32[]{:S(2)}) copy-start(s32[24]{0:T(128)} %model_ref.3) | copy-start | bytes 292
  7.2 68.0 %copy-start.20 = (s32[24]{0:T(128)S(1)}, s32[24]{0:T(128)}, u32[]{:S(2)}) copy-start(s32[24]{0:T(128)} %hidden_ref.5) | copy-start | bytes 292
  7.2 67.9 %copy-start.1 = (f32[24,128,128]{2,1,0:T(8,128)S(1)}, f32[24,128,128]{2,1,0:T(8,128)}, u32[]{:S(2)}) copy-start(f32[24,128,128]{2,1,0:T(8,128)} %up_hbm.3) | copy-start | bytes 4718596
  7.2 67.9 %copy-start.9 = (f32[128,512]{1,0:T(8,128)S(1)}, f32[128,512]{1,0:T(8,128)}, u32[]{:S(2)}) copy-start(f32[128,512]{1,0:T(8,128)} %right_ref.1) | copy-start | bytes 786436
  7.2 67.9 %all-gather.3.cloned.1.call-start = ((), (), s32[]{:S(2)}) async-start(), calls=%async_computation.5 | async-start | bytes 4325376 | tf_op jit(solution)/shard_map/all_gather | solution.py:295
  25.6 13.2 %all-to-all-start.1 = ((f32[32,8,128]{2,1,0:T(8,128)}), f32[32,8,128]{2,1,0:T(8,128)S(1)}, u32[]{:S(2)}, u32[]{:S(2)}) async-start(f32[32,8,128]{2,1,0:T(8,128)} %broadcast_in_dim.17), calls=%async_computation.1 | async-start | bytes 262144 | tf_op jit(solution)/shard_map/all_to_all | solution.py:267
  75.2 1.4 copy-start.2
  76.6 0.9 copy-start.10
  89.9 11.8 %collective-permute-start = (f32[2,8,128,128]{3,2,1,0:T(8,128)}, f32[2,8,128,128]{3,2,1,0:T(8,128)S(1)}, u32[]{:S(2)}, u32[]{:S(2)}) collective-permute-start(f32[2,8,128,128]{3,2,1,0:T(8,128)} %get-tuple-element.37.after_hbm), channel_id=1, source_target_pairs={{0,1},{1,0},{2,3},{3,2},{4,5},{5,4},{6,7},{7,6},{8,9},{9,8},{10,11... | collective-permute-start | bytes 3145736 | tf_op jit(solution)/shard_map/ppermute | solution.py:263
  96.9 0.9 copy-start.3
  97.9 0.9 copy-start.5
  98.8 31.8 %collective-permute-start.8 = (f32[2,2,28,16,128]{4,3,2,1,0:T(8,128)}, f32[2,2,28,16,128]{4,3,2,1,0:T(8,128)}, u32[]{:S(2)}, u32[]{:S(2)}) collective-permute-start(f32[2,2,28,16,128]{4,3,2,1,0:T(8,128)} %get-tuple-element.50), channel_id=1, source_target_pairs={{0,192},{32,224},{64,128},{96,160},{128,64},{160,96},{192,0},{224,... | collective-permute-start | bytes 2752520 | tf_op jit(solution)/shard_map/ppermute | solution.py:263
  101.3 29.3 %collective-permute-start.7 = (f32[2,2,28,16,128]{4,3,2,1,0:T(8,128)}, f32[2,2,28,16,128]{4,3,2,1,0:T(8,128)}, u32[]{:S(2)}, u32[]{:S(2)}) collective-permute-start(f32[2,2,28,16,128]{4,3,2,1,0:T(8,128)} %get-tuple-element.38.after_hbm), channel_id=1, source_target_pairs={{0,64},{32,96},{64,0},{96,32},{128,192},{160,224},{192,128},{224,1... | collective-permute-start | bytes 2752520 | tf_op jit(solution)/shard_map/ppermute | solution.py:263
  101.9 28.8 %copy-start.4 = (f32[2,2,28,16,128]{4,3,2,1,0:T(8,128)S(1)}, f32[2,2,28,16,128]{4,3,2,1,0:T(8,128)}, u32[]{:S(2)}) copy-start(f32[2,2,28,16,128]{4,3,2,1,0:T(8,128)} %copy-done.3) | copy-start | bytes 2752516
  101.9 28.8 %copy-start.6 = (f32[2,2,28,16,128]{4,3,2,1,0:T(8,128)S(1)}, f32[2,2,28,16,128]{4,3,2,1,0:T(8,128)}, u32[]{:S(2)}) copy-start(f32[2,2,28,16,128]{4,3,2,1,0:T(8,128)} %copy-done.5) | copy-start | bytes 2752516
  101.9 10.8 %collective-permute-start.1 = (f32[6,128,128]{2,1,0:T(8,128)S(1)}, f32[6,128,128]{2,1,0:T(8,128)S(1)}, u32[]{:S(2)}, u32[]{:S(2)}) collective-permute-start(f32[6,128,128]{2,1,0:T(8,128)S(1)} %get-tuple-element.40), channel_id=1, source_target_pairs={{0,2},{1,3},{2,0},{3,1},{4,6},{5,7},{6,4},{7,5},{8,10},{9,11},{10,... | collective-permute-start | bytes 1179656 | tf_op jit(solution)/shard_map/ppermute | solution.py:263
  103.2 10.5 %collective-permute-start.2 = (f32[6,128,128]{2,1,0:T(8,128)S(1)}, f32[6,128,128]{2,1,0:T(8,128)S(1)}, u32[]{:S(2)}, u32[]{:S(2)}) collective-permute-start(f32[6,128,128]{2,1,0:T(8,128)S(1)} %get-tuple-element.41), channel_id=1, source_target_pairs={{0,6},{1,7},{2,4},{3,5},{4,2},{5,3},{6,0},{7,1},{8,14},{9,15},{10,... | collective-permute-start | bytes 1179656 | tf_op jit(solution)/shard_map/ppermute | solution.py:263
  114.4 11.4 %copy-start.17 = (f32[4,128,128]{2,1,0:T(8,128)}, f32[4,128,128]{2,1,0:T(8,128)S(1)}, u32[]{:S(2)}) copy-start(f32[4,128,128]{2,1,0:T(8,128)S(1)} %get-tuple-element.43.after_hbm) | copy-start | bytes 786436
  114.4 10.0 %collective-permute-start.4 = (f32[4,128,128]{2,1,0:T(8,128)}, f32[4,128,128]{2,1,0:T(8,128)S(1)}, u32[]{:S(2)}, u32[]{:S(2)}) collective-permute-start(f32[4,128,128]{2,1,0:T(8,128)} %get-tuple-element.44), channel_id=1, source_target_pairs={{0,2},{1,3},{2,0},{3,1},{4,6},{5,7},{6,4},{7,5},{8,10},{9,11},{10,... | collective-permute-start | bytes 786440 | tf_op jit(solution)/shard_map/ppermute | solution.py:263
  116.5 8.6 %collective-permute-start.3 = (f32[4,128,128]{2,1,0:T(8,128)S(1)}, f32[4,128,128]{2,1,0:T(8,128)S(1)}, u32[]{:S(2)}, u32[]{:S(2)}) collective-permute-start(f32[4,128,128]{2,1,0:T(8,128)S(1)} %get-tuple-element.43.after_hbm), channel_id=1, source_target_pairs={{0,6},{1,7},{2,4},{3,5},{4,2},{5,3},{6,0},{7,1},{8,14},{9,15},{10,... | collective-permute-start | bytes 786440 | tf_op jit(solution)/shard_map/ppermute | solution.py:263
  117.5 16.6 %all-to-all-start.2 = ((f32[32,8,128]{2,1,0:T(8,128)}), f32[32,8,128]{2,1,0:T(8,128)S(1)}, u32[]{:S(2)}, u32[]{:S(2)}) async-start(f32[32,8,128]{2,1,0:T(8,128)} %bitcast.9), calls=%async_computation.2 | async-start | bytes 262144 | tf_op jit(solution)/shard_map/all_to_all | solution.py:267
  124.4 0.7 copy-start.13
  125.1 0.7 copy-start.15
  125.8 1.0 copy-start.14
  126.7 0.9 copy-start.16
  128.4 0.7 copy-start.11
  129.1 14.5 %collective-permute-start.5 = (f32[2,2,128,128]{3,2,1,0:T(8,128)}, f32[2,2,128,128]{3,2,1,0:T(8,128)}, u32[]{:S(2)}, u32[]{:S(2)}) collective-permute-start(f32[2,2,128,128]{3,2,1,0:T(8,128)} %get-tuple-element.46), channel_id=1, source_target_pairs={{0,8},{1,9},{2,10},{3,11},{4,12},{5,13},{6,14},{7,15},{8,0},{9,1},... | collective-permute-start | bytes 786440 | tf_op jit(solution)/shard_map/ppermute | solution.py:263
  130.7 1.0 copy-start.18
  133.3 0.8 copy-start.21
  134.8 25.1 %copy-start.12 = (f32[2,2,128,128]{3,2,1,0:T(8,128)S(1)}, f32[2,2,128,128]{3,2,1,0:T(8,128)}, u32[]{:S(2)}) copy-start(f32[2,2,128,128]{3,2,1,0:T(8,128)} %copy-done.11) | copy-start | bytes 786436
  134.8 12.7 %all-to-all-start.3 = ((f32[32,8,128]{2,1,0:T(8,128)}), f32[32,8,128]{2,1,0:T(8,128)S(1)}, u32[]{:S(2)}, u32[]{:S(2)}) async-start(f32[32,8,128]{2,1,0:T(8,128)} %pieces.1), calls=%async_computation.3 | async-start | bytes 262144 | tf_op jit(solution)/shard_map/all_to_all | solution.py:267
  141.7 19.1 %copy-start.7 = (f32[128,128]{1,0:T(8,128)S(1)}, f32[128,128]{1,0:T(8,128)}, u32[]{:S(2)}) copy-start(f32[128,128]{1,0:T(8,128)} %grad_ref.1) | copy-start | bytes 196612
  141.7 19.1 %copy-start.8 = (f32[128,128]{1,0:T(8,128)S(1)}, f32[128,128]{1,0:T(8,128)}, u32[]{:S(2)}) copy-start(f32[128,128]{1,0:T(8,128)} %inputs_ref.1) | copy-start | bytes 196612
  141.7 13.9 %collective-permute-start.9 = (f32[2,28,16,128]{3,2,1,0:T(8,128)S(1)}, f32[2,28,16,128]{3,2,1,0:T(8,128)S(1)}, u32[]{:S(2)}, u32[]{:S(2)}) collective-permute-start(f32[2,28,16,128]{3,2,1,0:T(8,128)S(1)} %get-tuple-element.51.after_hbm), channel_id=1, source_target_pairs={{0,192},{32,224},{64,128},{96,160},{128,64},{160,96},{192,0},{224,... | collective-permute-start | bytes 1376264 | tf_op jit(solution)/shard_map/ppermute | solution.py:263
  142.8 12.5 %collective-permute-start.10 = (f32[2,28,16,128]{3,2,1,0:T(8,128)}, f32[2,28,16,128]{3,2,1,0:T(8,128)S(1)}, u32[]{:S(2)}, u32[]{:S(2)}) collective-permute-start(f32[2,28,16,128]{3,2,1,0:T(8,128)} %copy-done.21), channel_id=1, source_target_pairs={{0,64},{32,96},{64,0},{96,32},{128,192},{160,224},{192,128},{224,1... | collective-permute-start | bytes 1376264 | tf_op jit(solution)/shard_map/ppermute | solution.py:263
  144.6 15.2 %collective-permute-start.6 = (f32[2,128,128]{2,1,0:T(8,128)S(1)}, f32[2,128,128]{2,1,0:T(8,128)}, u32[]{:S(2)}, u32[]{:S(2)}) collective-permute-start(f32[2,128,128]{2,1,0:T(8,128)S(1)} %fusion.after_hbm), channel_id=1, source_target_pairs={{0,16},{1,17},{2,18},{3,19},{4,20},{5,21},{6,22},{7,23},{8,24},{9,... | collective-permute-start | bytes 393224 | tf_op jit(solution)/shard_map/ppermute | solution.py:263
  155.7 30.3 %collective-permute-start.11 = (f32[2,28,16,128]{3,2,1,0:T(8,128)S(1)}, f32[2,28,16,128]{3,2,1,0:T(8,128)S(1)}, u32[]{:S(2)}, u32[]{:S(2)}) collective-permute-start(f32[2,28,16,128]{3,2,1,0:T(8,128)S(1)} %get-tuple-element.55), channel_id=1, source_target_pairs={{0,32},{32,0},{64,96},{96,64},{128,160},{160,128},{192,224},{224,1... | collective-permute-start | bytes 1376264 | tf_op jit(solution)/shard_map/ppermute | solution.py:263
  161.7 23.6 %all-to-all-start.4 = ((f32[8,2,16,128]{3,2,1,0:T(8,128)}), f32[8,2,16,128]{3,2,1,0:T(8,128)S(1)}, u32[]{:S(2)}, u32[]{:S(2)}) async-start(f32[8,2,16,128]{3,2,1,0:T(8,128)} %ends.1), calls=%async_computation.4 | async-start | bytes 262144 | tf_op jit(solution)/shard_map/all_to_all | solution.py:384
Sparse Core Ops, SparseCore 0:
  10.5 64.6 all-gather.2
